TPU v7x, 512 devices: a whole 4x4x16 slice. The times are simulated.
512 devices in a mesh: panel: 64 (over x, z), obs: 8 (over y, core).
Axes of the slice: x: 4, y: 4, z: 16, core: 2. Of those that a mesh axis runs over, the one named last changes fastest.
Arguments:
- donor: bfloat16 [512, 125, 4, 1024], P('panel', None, None, 'obs'), may hold values from -6 to 6
- donor_elem: int32 [8192], P('obs'), may hold values from 0 to 1023, as said below
- local_coords: float32 [3, 8192], P(None, 'obs'), may hold values from -1 to 1
- owner: int32 [8192], replicated, may hold values from 0 to 63, as said below
- weights: bfloat16 [1024, 4, 4, 8192], P('obs', None, None, 'panel'), may hold values from -0.015625 to 0.015625
- offsets: int32 [8, 64], P('obs', 'panel'), may hold values from 0 to 256
Outputs:
- pressure: float32 [512, 1024], P('panel', 'obs')
Inputs may be any that keep to these rules, and one draw needn't show every extreme that they name: `donor_elem`: point i lies in a donor element of the i // 1024-th block of 128 elements. Every owner owns exactly 128 points. Within each of the 8 aligned blocks of 1024 points an owner appears either 44 times or 128 / 8 - 128 / 32 times, and exactly one block holds 44 of its points.
All inputs are finite; a program needn't handle non-finite values.
Results may differ from a plain program's by a relative error of at most 0.0029.
Values may be sent and summed in bfloat16 or wider, within the bound.
A program may use at most 64 MiB of HBM per device.

v0:
```python
import jax
import jax.numpy as jnp
from jax import lax
from jax.sharding import PartitionSpec as P

BAND = 4
OBLK = 128
PTILE = 128
NODE_SPOTS = (-1.0, -0.5, 0.0, 0.5, 1.0)


def lagrange_table(coords):
    factors = []
    for direction in range(3):
        coord_row = coords[direction]
        columns = []
        for node_one in range(5):
            weighting = jnp.ones_like(coord_row)
            for node_two in range(5):
                if node_two != node_one:
                    weighting = weighting * (
                        (coord_row - NODE_SPOTS[node_two])
                        / (NODE_SPOTS[node_one] - NODE_SPOTS[node_two])
                    )
            columns.append(weighting)
        factors.append(jnp.stack(columns))
    node_table = (
        factors[0][:, None, None, :] * factors[1][None, :, None, :] * factors[2][None, None, :, :]
    )
    return node_table.reshape(125, coords.shape[1])


def body(donor, donor_elem, local_coords, owner, weights, offsets):
    share_index = lax.axis_index("obs")
    elem_local = donor_elem - share_index * donor.shape[3]
    node_table = lagrange_table(local_coords)

    def one_time(moment):
        values = jnp.take(moment, elem_local, axis=2)
        return jnp.sum(node_table[:, None, :] * values, axis=0).astype(jnp.bfloat16)

    local_sources = lax.map(one_time, donor)
    order = jnp.argsort(owner, stable=True)
    everything = lax.all_gather(local_sources, "obs", axis=2, tiled=True)
    outgoing = jnp.take(everything, order, axis=2)
    sources = lax.all_to_all(outgoing, "panel", split_axis=2, concat_axis=0, tiled=True)
    total_time = sources.shape[0]
    front = total_time // 2 + BAND - 1
    padded = jnp.pad(sources, ((front, 0), (0, 0), (0, 0)))
    delay_steps = offsets[0, 0]
    base = 0 + front - delay_steps
    stacked = jnp.stack(
        [lax.dynamic_slice_in_dim(padded, base - delay, total_time, 0) for delay in range(BAND)],
        axis=1,
    )
    stacked = stacked.reshape(total_time, BAND * padded.shape[1] * PTILE)
    weight_tile = weights
    weight_tile = weight_tile.reshape(OBLK, stacked.shape[1])
    running = lax.dot_general(
        stacked, weight_tile, (((1,), (1,)), ((), ())), preferred_element_type=jnp.float32
    )
    pressure = lax.psum_scatter(running, "panel", scatter_dimension=0, tiled=True)
    return pressure


def solution(mesh):
    return jax.shard_map(
        body,
        mesh=mesh,
        in_specs=(
            P("panel", None, None, "obs"),
            P("obs"),
            P(None, "obs"),
            P(),
            P("obs", None, None, "panel"),
            P("obs", "panel"),
        ),
        out_specs=P("panel", "obs"),
        check_vma=False,
    )
```

profile of v0, /device:TPU:8, one launch (start us, length us, event | category | flops | bytes accessed | tf_op | source)
XLA Modules:
  0.0 636.2 jit_solution(15393408633668595031)
XLA Ops:
  6.5 7.6 %sort.17 = (s32[8192]{0:T(1024)}, s32[8192]{0:T(1024)S(1)}) sort(s32[8192]{0:T(1024)} %param.11, s32[8192]{0:T(1024)S(1)} %iota.4), dimensions={0}, to_apply=%region_0.1 | sort | flops 106496 | bytes 131072 | tf_op jit(solution)/shard_map/jit(argsort)/sort | solution.py:43
  16.0 160.1 %while.11 = (s32[]{:T(128)}, bf16[8,4,1024]{2,0,1:T(8,128)(2,1)S(1)}, s32[1024]{0:T(1024)S(1)}, bf16[8,125,4,128]{3,2,1,0:T(4,128)(2,1)}, f32[5,1024]{1,0:T(8,12...) while((s32[]{:T(128)}, bf16[8,4,1024]{2,0,1:T(8,128)(2,1)S(1)}, s32[1024]{0:T(1024)S(1)}, ...), condition=%wide.region_3.4_spmd.clone, body=%wide.region_1.0_spmd.clone.sunk | while | flops 2182146 | bytes 6846565 | solution.py:42
  17.6 3.6 gather_fusion
  21.2 14.5 %fusion.23 = bf16[4,1024]{0,1:T(8,128)(2,1)S(1)} fusion(bf16[1024,125,4]{1,2,0:T(4,128)(2,1)S(1)} %gather_fusion, f32[125,1024]{0,1:T(8,128)S(1)} %copy.38, pred[1024]{0:T(1024)(128)(4,1)S(1)} %compare_and_fusion.3), kind=kLoop, calls=%fused_computation.4.clone.1 | loop fusion | flops 2043904 | bytes 1545216 | tf_op jit(solution)/shard_map/while/body/eval_jaxpr/reduce_sum | solution.py:40
  37.6 3.6 gather_fusion
  41.2 14.5 %fusion.23 = bf16[4,1024]{0,1:T(8,128)(2,1)S(1)} fusion(bf16[1024,125,4]{1,2,0:T(4,128)(2,1)S(1)} %gather_fusion, f32[125,1024]{0,1:T(8,128)S(1)} %copy.38, pred[1024]{0:T(1024)(128)(4,1)S(1)} %compare_and_fusion.3), kind=kLoop, calls=%fused_computation.4.clone.1 | loop fusion | flops 2043904 | bytes 1545216 | tf_op jit(solution)/shard_map/while/body/eval_jaxpr/reduce_sum | solution.py:40
  57.6 3.6 gather_fusion
  61.2 14.5 %fusion.23 = bf16[4,1024]{0,1:T(8,128)(2,1)S(1)} fusion(bf16[1024,125,4]{1,2,0:T(4,128)(2,1)S(1)} %gather_fusion, f32[125,1024]{0,1:T(8,128)S(1)} %copy.38, pred[1024]{0:T(1024)(128)(4,1)S(1)} %compare_and_fusion.3), kind=kLoop, calls=%fused_computation.4.clone.1 | loop fusion | flops 2043904 | bytes 1545216 | tf_op jit(solution)/shard_map/while/body/eval_jaxpr/reduce_sum | solution.py:40
  77.6 3.6 gather_fusion
  81.2 14.5 %fusion.23 = bf16[4,1024]{0,1:T(8,128)(2,1)S(1)} fusion(bf16[1024,125,4]{1,2,0:T(4,128)(2,1)S(1)} %gather_fusion, f32[125,1024]{0,1:T(8,128)S(1)} %copy.38, pred[1024]{0:T(1024)(128)(4,1)S(1)} %compare_and_fusion.3), kind=kLoop, calls=%fused_computation.4.clone.1 | loop fusion | flops 2043904 | bytes 1545216 | tf_op jit(solution)/shard_map/while/body/eval_jaxpr/reduce_sum | solution.py:40
  101.2 14.5 %fusion.23 = bf16[4,1024]{0,1:T(8,128)(2,1)S(1)} fusion(bf16[1024,125,4]{1,2,0:T(4,128)(2,1)S(1)} %gather_fusion, f32[125,1024]{0,1:T(8,128)S(1)} %copy.38, pred[1024]{0:T(1024)(128)(4,1)S(1)} %compare_and_fusion.3), kind=kLoop, calls=%fused_computation.4.clone.1 | loop fusion | flops 2043904 | bytes 1545216 | tf_op jit(solution)/shard_map/while/body/eval_jaxpr/reduce_sum | solution.py:40
  121.2 14.5 %fusion.23 = bf16[4,1024]{0,1:T(8,128)(2,1)S(1)} fusion(bf16[1024,125,4]{1,2,0:T(4,128)(2,1)S(1)} %gather_fusion, f32[125,1024]{0,1:T(8,128)S(1)} %copy.38, pred[1024]{0:T(1024)(128)(4,1)S(1)} %compare_and_fusion.3), kind=kLoop, calls=%fused_computation.4.clone.1 | loop fusion | flops 2043904 | bytes 1545216 | tf_op jit(solution)/shard_map/while/body/eval_jaxpr/reduce_sum | solution.py:40
  141.3 14.5 %fusion.23 = bf16[4,1024]{0,1:T(8,128)(2,1)S(1)} fusion(bf16[1024,125,4]{1,2,0:T(4,128)(2,1)S(1)} %gather_fusion, f32[125,1024]{0,1:T(8,128)S(1)} %copy.38, pred[1024]{0:T(1024)(128)(4,1)S(1)} %compare_and_fusion.3), kind=kLoop, calls=%fused_computation.4.clone.1 | loop fusion | flops 2043904 | bytes 1545216 | tf_op jit(solution)/shard_map/while/body/eval_jaxpr/reduce_sum | solution.py:40
  161.3 14.5 %fusion.23 = bf16[4,1024]{0,1:T(8,128)(2,1)S(1)} fusion(bf16[1024,125,4]{1,2,0:T(4,128)(2,1)S(1)} %gather_fusion, f32[125,1024]{0,1:T(8,128)S(1)} %copy.38, pred[1024]{0:T(1024)(128)(4,1)S(1)} %compare_and_fusion.3), kind=kLoop, calls=%fused_computation.4.clone.1 | loop fusion | flops 2043904 | bytes 1545216 | tf_op jit(solution)/shard_map/while/body/eval_jaxpr/reduce_sum | solution.py:40
  176.1 15.8 %all_gather.3 = bf16[8,4,8192]{2,0,1:T(8,128)(2,1)S(1)} all-gather(bf16[8,4,1024]{2,0,1:T(8,128)(2,1)S(1)} %get-tuple-element.34), channel_id=1, replica_groups=mesh['panel'=64,'obs'=8] {'obs'}, dimensions={2}, use_global_device_ids=true | all-gather | bytes 589824 | tf_op jit(solution)/shard_map/all_gather | solution.py:44
  191.9 8.1 %copy.24 = bf16[8,4,8192]{0,1,2:T(4,128)(2,1)} copy(bf16[8,4,8192]{2,0,1:T(8,128)(2,1)S(1)} %all_gather.3) | data formatting | bytes 1048576 | tf_op jit(solution)/shard_map/all_gather | solution.py:44
  200.0 59.6 %gather_fusion.1 = bf16[8192,8,4]{1,2,0:T(4,128)(2,1)} fusion(bf16[8,4,8192]{0,1,2:T(4,128)(2,1)} %copy.24, s32[8192]{0:T(1024)S(1)} %fusion.19), kind=kCustom, calls=%fused_computation.1 | custom fusion | bytes 1081344 | tf_op jit(solution)/shard_map/jit(_take)/gather | solution.py:45
  259.7 30.9 %fusion.21 = bf16[8192,4,8]{2,1,0:T(4,128)(2,1)} fusion(bf16[8192,8,4]{1,2,0:T(4,128)(2,1)} %gather_fusion.1, pred[8192]{0:T(1024)(128)(4,1)S(1)} %compare_and_fusion.1), kind=kLoop, calls=%fused_computation.65 | loop fusion | flops 262144 | bytes 1056768
  290.6 11.2 %reshape.84 = bf16[64,2,2048]{2,1,0:T(2,128)(2,1)} reshape(bf16[8192,4,8]{2,1,0:T(4,128)(2,1)} %fusion.21) | data formatting | bytes 1048576
  301.8 16.1 %all-to-all-start = ((bf16[64,2,2048]{2,1,0:T(2,128)(2,1)}), bf16[64,2,2048]{2,1,0:T(2,128)(2,1)S(1)}, u32[]{:S(2)}, u32[]{:S(2)}) async-start(bf16[64,2,2048]{2,1,0:T(2,128)(2,1)} %reshape.84), calls=%async_computation | async-start | bytes 1048576 | tf_op jit(solution)/shard_map/all_to_all | solution.py:46
  318.8 31.5 %all-to-all-done = bf16[64,2,2048]{2,1,0:T(2,128)(2,1)S(1)} async-done(((bf16[64,2,2048]{2,1,0:T(2,128)(2,1)}), bf16[64,2,2048]{2,1,0:T(2,128)(2,1)S(1)}, u32[]{:S(2)}, u32[]{:S(2)}) %all-to-all-start) | async-done | bytes 524320 | tf_op jit(solution)/shard_map/all_to_all | solution.py:46
  350.3 10.9 %reshape.85 = bf16[8192,4,8]{2,1,0:T(4,128)(2,1)} reshape(bf16[64,2,2048]{2,1,0:T(2,128)(2,1)S(1)} %all-to-all-done) | data formatting | bytes 1048576
  361.1 9.9 %copy.25 = bf16[64,8,4,128]{3,1,0,2:T(8,128)(2,1)S(1)} copy(bf16[64,8,4,128]{1,2,3,0:T(4,128)(2,1)} %bitcast.53) | data formatting | bytes 1048576 | tf_op jit(solution)/shard_map/all_to_all | solution.py:46
  375.3 252.8 %all-reduce.4.cloned.1.call-done = f32[512,128]{1,0:T(8,128)} async-done(((f32[512,128]{1,0:T(8,128)}), f32[512,128]{1,0:T(8,128)}) %all-reduce.4.cloned.1.call-update) | async-done | bytes 262160
  (102 shorter events, 36.1 us)
Async XLA Ops:
  6.5 365.4 %copy-start = (bf16[128,4,4,128]{3,2,1,0:T(4,128)(2,1)S(1)}, bf16[128,4,4,128]{3,2,1,0:T(4,128)(2,1)}, u32[]{:S(2)}) copy-start(bf16[128,4,4,128]{3,2,1,0:T(4,128)(2,1)} %param.12) | copy-start | bytes 1572868
  301.8 48.5 %all-to-all-start = ((bf16[64,2,2048]{2,1,0:T(2,128)(2,1)}), bf16[64,2,2048]{2,1,0:T(2,128)(2,1)S(1)}, u32[]{:S(2)}, u32[]{:S(2)}) async-start(bf16[64,2,2048]{2,1,0:T(2,128)(2,1)} %reshape.84), calls=%async_computation | async-start | bytes 1048576 | tf_op jit(solution)/shard_map/all_to_all | solution.py:46
  317.9 310.2 %all-reduce.4.cloned.1.call-start = ((), (), s32[]{:S(2)}) async-start(), calls=%async_computation.1 | async-start | bytes 524288
Sparse Core Ops, SparseCore 0:
  373.5 254.5 all-reduce.3
where the time goes:
time: 637 us; the launch traced here: 636 us
  waiting for transfers between devices  284 us (45%)
  other arithmetic  157 us (25%)
  local copies, waits for them, and re-layouts  146 us (23%)
  starting transfers between devices  16.3 us (3%)
  blocking collectives  15.8 us (2%)
  between operations  14.8 us (2%)
    unnamed x2, waiting for transfers between devices  253 us
    reduce_sum x8, other arithmetic, one_time(): return jnp.sum(node_table[:, None, :] * values, axis=0).astype(jnp.bfloat16)  116 us
    gather x1, local copies, waits for them, and re-layouts, body(): outgoing = jnp.take(everything, order, axis=2)  59.6 us
    all_to_all x1, waiting for transfers between devices, body(): lax.all_to_all(outgoing, 'panel', split_axis=2, concat_axis=0, tiled=True)  31.5 us
    unnamed x1, other arithmetic  30.9 us
    gather x8, local copies, waits for them, and re-layouts, one_time(): values = jnp.take(moment, elem_local, axis=2)  28.6 us
    unnamed x6, local copies, waits for them, and re-layouts  24.6 us
    all_to_all x1, starting transfers between devices, body(): lax.all_to_all(outgoing, 'panel', split_axis=2, concat_axis=0, tiled=True)  16.1 us
  transfers between devices with their start and end apart: 2, of which 2 were waited for; matrix products, arithmetic and copies ran while one was open for 0% of the time, Pallas kernels for 0%

commit v1 on v0

--- a/solution.py
+++ b/solution.py
@@ -41,7 +41,26 @@
 
     local_sources = lax.map(one_time, donor)
     order = jnp.argsort(owner, stable=True)
-    everything = lax.all_gather(local_sources, "obs", axis=2, tiled=True)
+    k_now = lax.axis_size("obs")
+    back = lax.axis_index("obs")
+    ready, current_arr, carry = (k_now, back, local_sources.shape[2])
+    line_up = [u * ready if tick == 2 else u for tick, u in enumerate(local_sources.shape)]
+    g_now = w_next = local_sources
+    everything = lax.dynamic_update_slice_in_dim(
+        jnp.zeros(line_up, local_sources.dtype), local_sources, current_arr * carry, axis=2
+    )
+    for ix in range(1, ready // 2 + 1):
+        g_now = lax.ppermute(g_now, "obs", [(tick, (tick + 1) % ready) for tick in range(ready)])
+        everything = lax.dynamic_update_slice_in_dim(
+            everything, g_now, (current_arr - ix) % ready * carry, axis=2
+        )
+        if 2 * ix < ready:
+            w_next = lax.ppermute(
+                w_next, "obs", [(tick, (tick - 1) % ready) for tick in range(ready)]
+            )
+            everything = lax.dynamic_update_slice_in_dim(
+                everything, w_next, (current_arr + ix) % ready * carry, axis=2
+            )
     outgoing = jnp.take(everything, order, axis=2)
     sources = lax.all_to_all(outgoing, "panel", split_axis=2, concat_axis=0, tiled=True)
     total_time = sources.shape[0]

time: 637 us -> 657 us (1.031)
  local copies, waits for them, and re-layouts: 146 us -> 172 us
  blocking collectives: 15.8 us -> 0 us
    all_gather x1 -> x0, blocking collectives: 15.8 us -> none  [body(): everything = lax.all_gather(local_sources, 'obs', axis=2, tiled=True)]
    dynamic_update_slice x0 -> x8, local copies, waits for them, and re-layouts: none -> 10.9 us  [the longest x4 5.45 us: body(): lax.dynamic_update_slice_in_dim(everything, g_now, (current_arr - ix) % r...]
    while x0 -> x2, local copies, waits for them, and re-layouts: none -> 10.2 us  [body(): local_sources = lax.map(one_time, donor)]
    ppermute x0 -> x7, starting transfers between devices: none -> 8.87 us  [the longest x3 8.85 us: body(): lax.ppermute(w_next, 'obs', [(tick, (tick - 1) % ready) for tick in range...]
    all_gather x1 -> x0, local copies, waits for them, and re-layouts: 8.11 us -> none  [body(): everything = lax.all_gather(local_sources, 'obs', axis=2, tiled=True)]
    unnamed x6 -> x8, local copies, waits for them, and re-layouts: 24.6 us -> 24.6 us
  transfers between devices with their start and end apart: 2 -> 9, of which waited for: 2 -> 3; matrix products, arithmetic and copies ran while one was open for 0% -> 5% of each run, Pallas kernels for 0% -> 0%
where the time goes in v1:
time: 657 us; the launch traced here: 656 us
  waiting for transfers between devices  288 us (44%)
  local copies, waits for them, and re-layouts  172 us (26%)
  other arithmetic  156 us (24%)
  starting transfers between devices  22.7 us (3%)
  between operations  14.9 us (2%)
    unnamed x2, waiting for transfers between devices  254 us
    reduce_sum x8, other arithmetic, one_time(): return jnp.sum(node_table[:, None, :] * values, axis=0).astype(jnp.bfloat16)  116 us
    gather x1, local copies, waits for them, and re-layouts, body(): outgoing = jnp.take(everything, order, axis=2)  59.7 us
    all_to_all x1, waiting for transfers between devices, body(): lax.all_to_all(outgoing, 'panel', split_axis=2, concat_axis=0, tiled=True)  31.1 us
    unnamed x1, other arithmetic  30.9 us
    gather x8, local copies, waits for them, and re-layouts, one_time(): values = jnp.take(moment, elem_local, axis=2)  28.6 us
    unnamed x8, local copies, waits for them, and re-layouts  24.6 us
    all_to_all x1, starting transfers between devices, body(): lax.all_to_all(outgoing, 'panel', split_axis=2, concat_axis=0, tiled=True)  13.8 us
  transfers between devices with their start and end apart: 9, of which 3 were waited for; matrix products, arithmetic and copies ran while one was open for 5% of the time, Pallas kernels for 0%

profile of v1, /device:TPU:8, one launch (start us, length us, event | category | flops | bytes accessed | tf_op | source)
XLA Modules:
  0.0 655.8 jit_solution(4042926453490158697)
XLA Ops:
  8.4 163.2 %while.11 = (s32[]{:T(128)}, bf16[8,4,1024]{1,2,0:T(8,128)(2,1)}, s32[1024]{0:T(1024)S(1)}, bf16[8,125,4,128]{3,2,1,0:T(4,128)(2,1)}, f32[5,1024]{1,0:T(8,128)S(1)}, /*index=5*/f32[5,5,1024]{2,1,0:T(8,128)S(1)}, s32[]{:T(128)}) while((s32[]{:T(128)}, bf16[8,4,1024]{1,2,0:T(8,128)(2,1)}, s32[1024]{0:T(1024)S(1)}, ...), condition=%wide.region_3.4_spmd.clone, body=%wide.region_1.0_spmd.clone.sunk | while | flops 2182146 | bytes 7084625 | solution.py:42
  9.5 3.6 gather_fusion
  13.5 14.5 %fusion.23 = bf16[4,1024]{0,1:T(8,128)(2,1)S(1)} fusion(bf16[1024,125,4]{1,2,0:T(4,128)(2,1)S(1)} %gather_fusion, f32[125,1024]{0,1:T(8,128)S(1)} %copy.49, pred[1024]{0:T(1024)(128)(4,1)S(1)} %compare_and_fusion.3), kind=kLoop, calls=%fused_computation.4.clone.1 | loop fusion | flops 2043904 | bytes 1545216 | tf_op jit(solution)/shard_map/while/body/eval_jaxpr/reduce_sum | solution.py:40
  33.9 14.5 %fusion.23 = bf16[4,1024]{0,1:T(8,128)(2,1)S(1)} fusion(bf16[1024,125,4]{1,2,0:T(4,128)(2,1)S(1)} %gather_fusion, f32[125,1024]{0,1:T(8,128)S(1)} %copy.49, pred[1024]{0:T(1024)(128)(4,1)S(1)} %compare_and_fusion.3), kind=kLoop, calls=%fused_computation.4.clone.1 | loop fusion | flops 2043904 | bytes 1545216 | tf_op jit(solution)/shard_map/while/body/eval_jaxpr/reduce_sum | solution.py:40
  50.3 3.6 gather_fusion
  54.3 14.5 %fusion.23 = bf16[4,1024]{0,1:T(8,128)(2,1)S(1)} fusion(bf16[1024,125,4]{1,2,0:T(4,128)(2,1)S(1)} %gather_fusion, f32[125,1024]{0,1:T(8,128)S(1)} %copy.49, pred[1024]{0:T(1024)(128)(4,1)S(1)} %compare_and_fusion.3), kind=kLoop, calls=%fused_computation.4.clone.1 | loop fusion | flops 2043904 | bytes 1545216 | tf_op jit(solution)/shard_map/while/body/eval_jaxpr/reduce_sum | solution.py:40
  70.7 3.6 gather_fusion
  74.7 14.5 %fusion.23 = bf16[4,1024]{0,1:T(8,128)(2,1)S(1)} fusion(bf16[1024,125,4]{1,2,0:T(4,128)(2,1)S(1)} %gather_fusion, f32[125,1024]{0,1:T(8,128)S(1)} %copy.49, pred[1024]{0:T(1024)(128)(4,1)S(1)} %compare_and_fusion.3), kind=kLoop, calls=%fused_computation.4.clone.1 | loop fusion | flops 2043904 | bytes 1545216 | tf_op jit(solution)/shard_map/while/body/eval_jaxpr/reduce_sum | solution.py:40
  95.1 14.5 %fusion.23 = bf16[4,1024]{0,1:T(8,128)(2,1)S(1)} fusion(bf16[1024,125,4]{1,2,0:T(4,128)(2,1)S(1)} %gather_fusion, f32[125,1024]{0,1:T(8,128)S(1)} %copy.49, pred[1024]{0:T(1024)(128)(4,1)S(1)} %compare_and_fusion.3), kind=kLoop, calls=%fused_computation.4.clone.1 | loop fusion | flops 2043904 | bytes 1545216 | tf_op jit(solution)/shard_map/while/body/eval_jaxpr/reduce_sum | solution.py:40
  115.5 14.5 %fusion.23 = bf16[4,1024]{0,1:T(8,128)(2,1)S(1)} fusion(bf16[1024,125,4]{1,2,0:T(4,128)(2,1)S(1)} %gather_fusion, f32[125,1024]{0,1:T(8,128)S(1)} %copy.49, pred[1024]{0:T(1024)(128)(4,1)S(1)} %compare_and_fusion.3), kind=kLoop, calls=%fused_computation.4.clone.1 | loop fusion | flops 2043904 | bytes 1545216 | tf_op jit(solution)/shard_map/while/body/eval_jaxpr/reduce_sum | solution.py:40
  135.9 14.5 %fusion.23 = bf16[4,1024]{0,1:T(8,128)(2,1)S(1)} fusion(bf16[1024,125,4]{1,2,0:T(4,128)(2,1)S(1)} %gather_fusion, f32[125,1024]{0,1:T(8,128)S(1)} %copy.49, pred[1024]{0:T(1024)(128)(4,1)S(1)} %compare_and_fusion.3), kind=kLoop, calls=%fused_computation.4.clone.1 | loop fusion | flops 2043904 | bytes 1545216 | tf_op jit(solution)/shard_map/while/body/eval_jaxpr/reduce_sum | solution.py:40
  156.3 14.5 %fusion.23 = bf16[4,1024]{0,1:T(8,128)(2,1)S(1)} fusion(bf16[1024,125,4]{1,2,0:T(4,128)(2,1)S(1)} %gather_fusion, f32[125,1024]{0,1:T(8,128)S(1)} %copy.49, pred[1024]{0:T(1024)(128)(4,1)S(1)} %compare_and_fusion.3), kind=kLoop, calls=%fused_computation.4.clone.1 | loop fusion | flops 2043904 | bytes 1545216 | tf_op jit(solution)/shard_map/while/body/eval_jaxpr/reduce_sum | solution.py:40
  175.3 8.2 %copy.27 = bf16[8,4,1024]{0,1,2:T(4,128)(2,1)S(1)} copy(bf16[8,4,1024]{1,2,0:T(8,128)(2,1)} %get-tuple-element.34) | data formatting | bytes 131072 | tf_op jit(solution)/shard_map/while | solution.py:42
  183.5 6.8 %sort.17 = (s32[8192]{0:T(1024)}, s32[8192]{0:T(1024)S(1)}) sort(s32[8192]{0:T(1024)S(1)} %copy-done.1, s32[8192]{0:T(1024)S(1)} %iota.4), dimensions={0}, to_apply=%region_0.1 | sort | flops 106496 | bytes 131072 | tf_op jit(solution)/shard_map/jit(argsort)/sort | solution.py:43
  190.3 5.4 broadcast_in_dim.34
  201.2 4.1 collective-permute-start.3
  221.2 59.7 %gather_fusion.1 = bf16[8192,8,4]{1,2,0:T(4,128)(2,1)} fusion(bf16[8,4,8192]{0,1,2:T(4,128)(2,1)} %constant_dynamic-update-slice_fusion, s32[8192]{0:T(1024)S(1)} %fusion.19), kind=kCustom, calls=%fused_computation.1 | custom fusion | bytes 1081344 | tf_op jit(solution)/shard_map/jit(_take)/gather | solution.py:64
  280.9 30.9 %fusion.21 = bf16[8192,4,8]{2,1,0:T(4,128)(2,1)} fusion(bf16[8192,8,4]{1,2,0:T(4,128)(2,1)} %gather_fusion.1, pred[8192]{0:T(1024)(128)(4,1)S(1)} %compare_and_fusion.1), kind=kLoop, calls=%fused_computation.73 | loop fusion | flops 262144 | bytes 1056768
  311.9 11.2 %reshape.84 = bf16[64,2,2048]{2,1,0:T(2,128)(2,1)} reshape(bf16[8192,4,8]{2,1,0:T(4,128)(2,1)} %fusion.21) | data formatting | bytes 1048576
  323.0 13.8 %all-to-all-start = ((bf16[64,2,2048]{2,1,0:T(2,128)(2,1)}), bf16[64,2,2048]{2,1,0:T(2,128)(2,1)S(1)}, u32[]{:S(2)}, u32[]{:S(2)}) async-start(bf16[64,2,2048]{2,1,0:T(2,128)(2,1)} %reshape.84), calls=%async_computation | async-start | bytes 1048576 | tf_op jit(solution)/shard_map/all_to_all | solution.py:65
  337.5 31.1 %all-to-all-done = bf16[64,2,2048]{2,1,0:T(2,128)(2,1)S(1)} async-done(((bf16[64,2,2048]{2,1,0:T(2,128)(2,1)}), bf16[64,2,2048]{2,1,0:T(2,128)(2,1)S(1)}, u32[]{:S(2)}, u32[]{:S(2)}) %all-to-all-start) | async-done | bytes 524320 | tf_op jit(solution)/shard_map/all_to_all | solution.py:65
  368.7 10.9 %reshape.85 = bf16[8192,4,8]{2,1,0:T(4,128)(2,1)} reshape(bf16[64,2,2048]{2,1,0:T(2,128)(2,1)S(1)} %all-to-all-done) | data formatting | bytes 1048576
  379.6 9.9 %copy.42 = bf16[8,4,64,128]{3,0,2,1:T(8,128)(2,1)S(1)} copy(bf16[8,4,64,128]{0,1,3,2:T(4,128)(2,1)} %bitcast.53) | data formatting | bytes 1048576 | tf_op jit(solution)/shard_map/all_to_all | solution.py:65
  393.7 254.0 %all-reduce.4.cloned.1.call-done = f32[512,128]{1,0:T(8,128)} async-done(((f32[512,128]{1,0:T(8,128)}), f32[512,128]{1,0:T(8,128)}) %all-reduce.4.cloned.1.call-update) | async-done | bytes 262160
  (126 shorter events, 67.7 us)
Async XLA Ops:
  6.5 383.8 %copy-start = (bf16[128,4,4,128]{3,2,1,0:T(4,128)(2,1)S(1)}, bf16[128,4,4,128]{3,2,1,0:T(4,128)(2,1)}, u32[]{:S(2)}) copy-start(bf16[128,4,4,128]{3,2,1,0:T(4,128)(2,1)} %param.12) | copy-start | bytes 1572868
  8.3 175.2 %copy-start.1 = (s32[8192]{0:T(1024)S(1)}, s32[8192]{0:T(1024)}, u32[]{:S(2)}) copy-start(s32[8192]{0:T(1024)} %param.11) | copy-start | bytes 98308
  173.6 23.5 %collective-permute-start = (bf16[8,4,1024]{2,0,1:T(8,128)(2,1)S(1)}, bf16[8,4,1024]{2,0,1:T(8,128)(2,1)S(1)}, u32[]{:S(2)}, u32[]{:S(2)}) collective-permute-start(bf16[8,4,1024]{2,0,1:T(8,128)(2,1)S(1)} %copy.28), channel_id=1, source_target_pairs={{0,1},{1,2},{2,3},{3,4},{4,5},{5,6},{6,7},{7,0},{8,9},{9,10},{10,1... | collective-permute-start | bytes 196616 | tf_op jit(solution)/shard_map/ppermute | solution.py:53
  173.6 25.6 %collective-permute-start.1 = (bf16[8,4,1024]{2,0,1:T(8,128)(2,1)S(1)}, bf16[8,4,1024]{2,0,1:T(8,128)(2,1)S(1)}, u32[]{:S(2)}, u32[]{:S(2)}) collective-permute-start(bf16[8,4,1024]{2,0,1:T(8,128)(2,1)S(1)} %copy.28), channel_id=1, source_target_pairs={{0,7},{1,0},{2,1},{3,2},{4,3},{5,4},{6,5},{7,6},{8,15},{9,8},{10,9... | collective-permute-start | bytes 196616 | tf_op jit(solution)/shard_map/ppermute | solution.py:58
  199.1 6.2 collective-permute-start.2
  201.2 6.1 collective-permute-start.3
  207.3 5.0 collective-permute-start.4
  209.3 5.0 collective-permute-start.5
  214.3 4.9 collective-permute-start.6
  323.0 45.6 %all-to-all-start = ((bf16[64,2,2048]{2,1,0:T(2,128)(2,1)}), bf16[64,2,2048]{2,1,0:T(2,128)(2,1)S(1)}, u32[]{:S(2)}, u32[]{:S(2)}) async-start(bf16[64,2,2048]{2,1,0:T(2,128)(2,1)} %reshape.84), calls=%async_computation | async-start | bytes 1048576 | tf_op jit(solution)/shard_map/all_to_all | solution.py:65
  336.8 310.9 %all-reduce.4.cloned.1.call-start = ((), (), s32[]{:S(2)}) async-start(), calls=%async_computation.1 | async-start | bytes 524288
Sparse Core Ops, SparseCore 0:
  391.9 255.7 all-reduce.3
